TPU v7x, 128 devices: a whole 4x4x4 slice. The times are simulated.
128 devices in a mesh: lon: 8 (over y, core), lat: 16 (over x, z).
Axes of the slice: x: 4, y: 4, z: 4, core: 2. Of those that a mesh axis runs over, the one named last changes fastest.
Arguments:
- tangent: float32 [5, 72, 16, 9216], P(None, None, 'lat', 'lon'), may hold values from -6 to 6
- adjoint: float32 [5, 72, 16, 9216], P(None, None, 'lat', 'lon'), may hold values from -6 to 6
- winds: float32 [2, 72, 16, 9216], P(None, None, 'lat', 'lon'), may hold values from -3 to 3
- cutoff: int32 [128], replicated, may hold values from 72 to 576, as said below
Outputs:
- tl_out: float32 [5, 72, 16, 9216], P(None, None, 'lat', 'lon')
- adj_out: float32 [5, 72, 16, 9216], P(None, None, 'lat', 'lon')
Inputs may be any that keep to these rules, and one draw needn't show every extreme that they name: `cutoff`: rows j with 32 <= j < 96 hold values from 288 to 576, and row 64 holds 576; the other rows hold values from 72 to 575, and row 0 holds 72.
All inputs are finite; a program needn't handle non-finite values.
Results may differ from a plain program's by a relative error of at most 0.00008.
Values sent between devices are 32-bit elements; how exact they have to be, the bound alone decides.
A program may use at most 128 MiB of HBM per device.

v0:
```python
import functools
import math

import jax
import jax.numpy as jnp
import numpy as np
from jax import lax
from jax.experimental import pallas as pl
from jax.experimental.pallas import tpu as pltpu
from jax.sharding import PartitionSpec as P

MESH = pl.DeviceIdType.MESH
F32 = jnp.float32
BF16 = jnp.bfloat16
ROWS = 8
PIECES = 8
LANES = 128
BLOCK = 256
SPAN = 512
KINDS = (0, 4, 1, 2, 3)
ORDER = (4, 3, 5, 2, 6, 1, 7)
ROOT = math.sqrt(0.5)


def split_table(nring):
    lag = np.arange(SPAN) - SPAN // 2
    count = nring // PIECES
    parts = []
    for kind in KINDS:
        wave = kind + PIECES * np.arange(count)
        angle = (wave[:, None] * lag[None, :] % nring) * (2.0 * np.pi / nring)
        forms = (np.cos,) if kind in (0, 4) else (np.cos, np.sin)
        weight = (1.0 if kind in (0, 4) else 2.0) / nring
        for form in forms:
            parts.append(weight * form(angle))
    return np.stack(parts).astype(np.float32)


def halves(value):
    high = value.astype(BF16)
    return high, (value - high.astype(F32)).astype(BF16)


def dot(a, b):
    return jnp.dot(a, b, preferred_element_type=F32)


def to_parts(x):
    s0, d0 = x[0] + x[4], x[0] - x[4]
    s1, d1 = x[1] + x[5], x[1] - x[5]
    s2, d2 = x[2] + x[6], x[2] - x[6]
    s3, d3 = x[3] + x[7], x[3] - x[7]
    even, odd = s0 + s2, s1 + s3
    p, q = (d1 - d3) * ROOT, (d1 + d3) * ROOT
    return (even + odd, even - odd, d0 + p, -d2 - q, s0 - s2, s3 - s1, d0 - p, d2 - q)


def from_parts(z):
    a, b = z[0] + z[1], z[0] - z[1]
    even = (a + z[4], b - z[5], a - z[4], b + z[5])
    p, q = (z[2] - z[6]) * ROOT, (z[3] + z[7]) * ROOT
    odd = (z[2] + z[6], p - q, z[7] - z[3], -p - q)
    return [e + o for e, o in zip(even, odd)] + [e - o for e, o in zip(even, odd)]


def kernel(
    dims,
    cut_ref,
    table_hbm,
    tan_hbm,
    adj_hbm,
    wind_hbm,
    tl_out,
    adj_out,
    tan_v,
    wind_v,
    moved_v,
    damped_v,
    result_v,
    got_a,
    got_t,
    back_a,
    back_t,
    south_t,
    north_t,
    south_d,
    north_d,
    south_w,
    wind_row,
    line_t,
    line_d,
    edge_t,
    edge_d,
    table_v,
    lag_v,
    mat_high,
    mat_low,
    part_high,
    part_low,
    image_v,
    local_sem,
    fwd_a_send,
    fwd_a_recv,
    fwd_t_send,
    fwd_t_recv,
    back_a_send,
    back_a_recv,
    back_t_send,
    back_t_recv,
    edge_send,
    edge_recv,
    row_send,
    row_recv,
):
    fields, levels, share, slot = dims
    chans = fields * levels
    groups = levels // 8
    tiles = ROWS * 144 // LANES
    size, room = share * tiles, slot * tiles
    me = lax.axis_index("lon")
    band = lax.axis_index("lat")
    bands = lax.axis_size("lat")
    west, east = lax.rem(me + PIECES - 1, PIECES), lax.rem(me + 1, PIECES)
    south, north = lax.rem(band + bands - 1, bands), lax.rem(band + 1, bands)
    lane = lax.broadcasted_iota(jnp.int32, (8, LANES), 1)
    in16 = lane % 16
    sub = lane // 16

    barrier = pltpu.get_barrier_semaphore()
    for step in range(1, PIECES):
        pl.semaphore_signal(
            barrier, inc=1, device_id={"lon": lax.rem(me + step, PIECES)}, device_id_type=MESH
        )
    for other in (south, north):
        pl.semaphore_signal(barrier, inc=1, device_id={"lat": other}, device_id_type=MESH)

    load_tan = pltpu.make_async_copy(tan_hbm, tan_v, local_sem.at[0])
    load_wind = pltpu.make_async_copy(wind_hbm, wind_v, local_sem.at[1])
    load_table = pltpu.make_async_copy(table_hbm, table_v, local_sem.at[2])
    own_a = pltpu.make_async_copy(
        adj_hbm.at[pl.ds(me * size, size)], got_a.at[pl.ds(me * room, size)], local_sem.at[4]
    )
    load_tan.start()
    load_wind.start()
    own_a.start()
    load_table.start()

    def tile_of(ref, row, stride=tiles, count=8):
        return ref[pl.ds(row, count, stride=stride), :]

    def pack(source, wind, edge, line):
        planes = fields + (1 if wind is not None else 0)

        def body(lg, carry):
            first, last = list(carry[0]), list(carry[1])
            for f in range(planes):
                if f < fields:
                    at = (f * groups + lg) * 8
                    t = [tile_of(source, at * tiles + k) for k in range(tiles)]
                    for k in range(2):
                        line[0, pl.ds(k * chans + at, 8), :] = t[k]
                        line[1, pl.ds(k * chans + at, 8), :] = t[k + tiles - 2]
                else:
                    t = [tile_of(wind, lg * 8 * tiles + k) for k in range(tiles)]
                    for k in range(2):
                        wind_row[pl.ds(k * levels + lg * 8, 8), :] = tile_of(
                            wind, (groups + lg) * 8 * tiles + k + tiles - 2
                        )
                a, b = t[0], t[1]
                for r in range(1, ROWS):
                    a = jnp.where(sub == r, t[r], a)
                    b = jnp.where(sub == r, t[r + 1], b)
                here = in16 == lg
                first[f] = jnp.where(here, pltpu.roll(a, lg, 1), first[f])
                last[f] = jnp.where(here, pltpu.roll(b, lg + (LANES - 15), 1), last[f])
            return tuple(first), tuple(last)

        zero = tuple(jnp.zeros((8, LANES), F32) for _ in range(planes))
        first, last = lax.fori_loop(0, groups, body, (zero, zero))
        for f in range(planes):
            edge[0, 8 * f : 8 * f + 8, :] = first[f]
            edge[1, 8 * f : 8 * f + 8, :] = last[f]

    def edges(edge, at):
        return [
            pltpu.make_async_remote_copy(
                edge.at[0], edge.at[3], edge_send.at[at, 0], edge_recv.at[at, 0],
                device_id={"lon": west}, device_id_type=MESH,
            ),
            pltpu.make_async_remote_copy(
                edge.at[1], edge.at[2], edge_send.at[at, 1], edge_recv.at[at, 1],
                device_id={"lon": east}, device_id_type=MESH,
            ),
        ]

    def rows(line, to_south, to_north, at):
        return [
            pltpu.make_async_remote_copy(
                line.at[0], to_south, row_send.at[at, 0], row_recv.at[at, 0],
                device_id={"lat": south}, device_id_type=MESH,
            ),
            pltpu.make_async_remote_copy(
                line.at[1], to_north, row_send.at[at, 1], row_recv.at[at, 1],
                device_id={"lat": north}, device_id_type=MESH,
            ),
        ]

    def stencil(source, edge, from_south, from_north, target, sign):
        has_south = jnp.where(band > 0, 0.5, 0.0).astype(F32)
        has_north = jnp.where(band < bands - 1, 0.5, 0.0).astype(F32)

        def left(x, n):
            return pltpu.roll(x, LANES - n, 1)

        def body(lg, _):
            u = [tile_of(wind_v, lg * 8 * tiles + k) * 0.5 for k in range(tiles)]
            v = [tile_of(wind_v, (groups + lg) * 8 * tiles + k) for k in range(tiles)]
            v = [x * 0.5 for x in v[:-2]] + [v[-2] * jnp.where(lane >= 112, has_north, 0.5), v[-1] * has_north]
            v = [south_w[pl.ds(k * levels + lg * 8, 8), :] * has_south for k in range(2)] + v
            u_west = pltpu.roll(edge_t[2, 8 * fields : 8 * fields + 8, :], LANES - lg, 1) * 0.5
            for f in range(fields):
                at = (f * groups + lg) * 8
                t = [tile_of(source, at * tiles + k) for k in range(tiles)]
                far_west = pltpu.roll(edge[2, 8 * f : 8 * f + 8, :], LANES - lg, 1)
                far_east = pltpu.roll(edge[3, 8 * f : 8 * f + 8, :], 15 - lg, 1)
                shifted = [left(x, 1) for x in t]
                flux = []
                for k in range(tiles):
                    nxt = jnp.where(lane == 127, shifted[k + 1], shifted[k]) if k + 1 < tiles else shifted[k]
                    if k >= 1:
                        nxt = jnp.where(lane == 16 * (k - 1) + 15, far_east, nxt)
                    flux.append(u[k] * (t[k] + sign * nxt))
                turned = [pltpu.roll(x, 1, 1) for x in flux]
                out = []
                for k in range(tiles):
                    prev = jnp.where(lane == 0, turned[k - 1], turned[k]) if k >= 1 else turned[k]
                    if k < ROWS:
                        prev = jnp.where(lane == 16 * k, u_west * (far_west + sign * t[k]), prev)
                    out.append(t[k] - flux[k] + sign * prev)
                ext = [from_south[pl.ds(k * chans + at, 8), :] for k in range(2)] + t
                ext = ext + [from_north[pl.ds(k * chans + at, 8), :] for k in range(2)]
                shifted = [left(x, 16) for x in ext]
                flux = []
                for k in range(tiles + 2):
                    nxt = jnp.where(lane < 112, shifted[k + 1], shifted[k + 2])
                    flux.append(v[k] * (ext[k] + sign * nxt))
                turned = [pltpu.roll(x, 16, 1) for x in flux]
                for k in range(tiles):
                    prev = jnp.where(lane >= 16, turned[k + 1], turned[k])
                    target[pl.ds(at * tiles + k, 8, stride=tiles), :] = out[k] - flux[k + 2] + sign * prev
            return 0

        lax.fori_loop(0, groups, body, 0)

    def matrices():
        grow = lax.broadcasted_iota(jnp.int32, (8, 144), 0)
        limit = jnp.zeros((8, 144), F32)
        for r in range(ROWS):
            limit = jnp.where(grow == r, cut_ref[band * ROWS + r].astype(F32), limit)
        column = lax.broadcasted_iota(jnp.int32, (8, 144), 1)
        nring = PIECES * 144
        part = 0
        for kind in KINDS:
            wave = column * PIECES + kind
            wave = jnp.minimum(wave, jnp.abs(nring - wave)).astype(F32)
            ratio = limit / jnp.maximum(wave, 1.0)
            gain = jnp.where(wave <= limit, 1.0, ratio * ratio)
            high, low = halves(gain)
            both = jnp.concatenate([high, low], axis=0)
            for _ in range(1 if kind in (0, 4) else 2):
                table_high, table_low = halves(table_v[part])
                one = dot(both, table_high)
                two = dot(both, table_low)
                lag_v[part] = one[:8] + one[8:] + two[:8]
                part += 1

        wide = lax.broadcasted_iota(jnp.int32, (16, BLOCK), 1)

        def body(r, _):
            inside = (wide >= 16 * r) & (wide < 16 * r + 144)
            nought = jnp.zeros((16, PIECES * BLOCK), BF16)
            for a in range(9, 16):
                row = lax.rem(r + a, 16) * 16
                mat_high[r, pl.ds(row, 16), :] = nought
                mat_low[r, pl.ds(row, 16), :] = nought
            for part in range(PIECES):
                line = jnp.broadcast_to(lag_v[part, pl.ds(r, 1), :], (16, SPAN))
                strip = pltpu.roll(line, 0, 1, stride=1, stride_axis=0)
                strip = pltpu.roll(strip, 16 * r + (SPAN - 128), 1)
                for a in range(9):
                    block = jnp.where(inside, strip[:, 128 - 16 * a : 384 - 16 * a], 0.0)
                    high, low = halves(block)
                    row = (r + a) * 16
                    mat_high[r, pl.ds(row, 16), part * BLOCK : (part + 1) * BLOCK] = high
                    mat_low[r, pl.ds(row, 16), part * BLOCK : (part + 1) * BLOCK] = low
            return 0

        lax.fori_loop(0, ROWS, body, 0)

    def damp(got, back):
        def forward(p, _):
            for t in range(tiles):
                x = [got[pl.ds(c * room + p * 16 * tiles + t, 16, stride=tiles), :] for c in range(PIECES)]
                for k, y in enumerate(to_parts(x)):
                    high, low = halves(y)
                    part_high[k, pl.ds(p * 16, 16), t * LANES : (t + 1) * LANES] = high
                    part_low[k, pl.ds(p * 16, 16), t * LANES : (t + 1) * LANES] = low
            return 0

        lax.fori_loop(0, slot // 16, forward, 0)
        image_v[:, :, 0:LANES] = jnp.zeros((PIECES, slot, LANES), F32)

        def multiply(r, _):
            window = pl.ds(pl.multiple_of(r * LANES, LANES), BLOCK)
            this = pl.ds(pl.multiple_of(r * LANES, LANES), LANES)
            following = pl.ds(pl.multiple_of(r * LANES + LANES, LANES), LANES)

            def product(first, count):
                high = part_high[first : first + count, :, window].reshape(count * slot, BLOCK)
                low = part_low[first : first + count, :, window].reshape(count * slot, BLOCK)
                cols = slice(first * BLOCK, (first + count) * BLOCK)
                wide_high, wide_low = mat_high[r, :, cols], mat_low[r, :, cols]
                return dot(high, wide_high) + dot(low, wide_high) + dot(high, wide_low)

            def put(k, z):
                image_v[k, :, this] = image_v[k, :, this] + z[:, :LANES]
                image_v[k, :, following] = z[:, LANES:]

            put(0, product(0, 1))
            put(1, product(1, 1))
            for k in (2, 4, 6):
                z = product(k, 2)
                put(k, z[:slot, :BLOCK] - z[slot:, BLOCK:])
                put(k + 1, z[:slot, BLOCK:] + z[slot:, :BLOCK])
            return 0

        lax.fori_loop(0, ROWS, multiply, 0)

        def inverse(p, _):
            for t in range(tiles):
                z = [image_v[k, pl.ds(p * 8, 8), t * LANES : (t + 1) * LANES] for k in range(PIECES)]
                for c, x in enumerate(from_parts(z)):
                    back[pl.ds(c * room + p * 8 * tiles + t, 8, stride=tiles), :] = x
            return 0

        lax.fori_loop(0, slot // 8, inverse, 0)

    def scatter(source, got, send, recv):
        out = []
        for step in ORDER:
            to = lax.rem(me + step, PIECES)
            out.append(
                pltpu.make_async_remote_copy(
                    source.at[pl.ds(to * size, size)], got.at[pl.ds(me * room, size)],
                    send.at[step], recv.at[step], device_id={"lon": to}, device_id_type=MESH,
                )
            )
        return out

    def bring(back, target, send, recv):
        out = []
        for step in ORDER:
            to = lax.rem(me + step, PIECES)
            out.append(
                pltpu.make_async_remote_copy(
                    back.at[pl.ds(to * room, size)], target.at[pl.ds(me * size, size)],
                    send.at[step], recv.at[step], device_id={"lon": to}, device_id_type=MESH,
                )
            )
        return out

    def start(copies):
        for c in copies:
            c.start()

    def wait_recv(copies):
        for c in copies:
            c.wait_recv()

    def wait_send(copies):
        for c in copies:
            c.wait_send()

    load_tan.wait()
    load_wind.wait()
    pack(
        tan_v, wind_v, edge_t, line_t
    )
    pl.semaphore_wait(barrier, PIECES + 1)

    edges_t = edges(edge_t, 0)
    start(edges_t)
    send_a = scatter(adj_hbm, got_a, fwd_a_send, fwd_a_recv)
    start(send_a)
    rows_t = rows(line_t, north_t, south_t, 0)
    rows_w = pltpu.make_async_remote_copy(
        wind_row, south_w,
        row_send.at[2, 0], row_recv.at[2, 0], device_id={"lat": north}, device_id_type=MESH,
    )
    start(rows_t)
    rows_w.start()

    load_table.wait()
    matrices()

    wait_recv(edges_t)
    wait_recv(rows_t)
    rows_w.wait_recv()
    stencil(tan_v, edge_t, south_t, north_t, moved_v, 1.0)
    send_t = scatter(moved_v, got_t, fwd_t_send, fwd_t_recv)
    start(send_t)
    own_t = pltpu.make_async_copy(
        moved_v.at[pl.ds(me * size, size)], got_t.at[pl.ds(me * room, size)], local_sem.at[5]
    )
    own_t.start()

    own_a.wait()
    wait_recv(send_a)
    damp(got_a, back_a)
    home_a = bring(back_a, damped_v, back_a_send, back_a_recv)
    start(home_a)
    keep_a = pltpu.make_async_copy(
        back_a.at[pl.ds(me * room, size)], damped_v.at[pl.ds(me * size, size)], local_sem.at[6]
    )
    keep_a.start()

    own_t.wait()
    wait_recv(send_t)
    damp(got_t, back_t)

    keep_a.wait()
    wait_recv(home_a)
    pack(damped_v, None, edge_d, line_d)
    edges_d = edges(edge_d, 1)
    start(edges_d)
    rows_d = rows(line_d, north_d, south_d, 1)
    start(rows_d)
    home_t = bring(back_t, tl_out, back_t_send, back_t_recv)
    start(home_t)
    keep_t = pltpu.make_async_copy(
        back_t.at[pl.ds(me * room, size)], tl_out.at[pl.ds(me * size, size)], local_sem.at[7]
    )
    keep_t.start()

    wait_recv(edges_d)
    wait_recv(rows_d)
    stencil(damped_v, edge_d, south_d, north_d, result_v, -1.0)
    store = pltpu.make_async_copy(result_v, adj_out, local_sem.at[8])
    store.start()

    for copies in (edges_t, send_a, rows_t, send_t, home_a, edges_d, rows_d):
        wait_send(copies)
    rows_w.wait_send()
    keep_t.wait()
    store.wait()
    for c in home_t:
        c.wait()


def shards(tangent, adjoint, winds, cutoff):
    fields, levels, single, cells = tangent.shape
    chans = fields * levels
    share = chans // PIECES
    slot = -(-share // 16) * 16
    tiles = cells // LANES
    table = split_table(PIECES * cells // ROWS)
    state = jax.ShapeDtypeStruct((chans * tiles, LANES), F32)
    any_space = pl.BlockSpec(memory_space=pl.ANY)
    vmem = pltpu.VMEM
    dma = pltpu.SemaphoreType.DMA
    whole = vmem((chans * tiles, LANES), F32)
    tl, adj = pl.pallas_call(
        functools.partial(kernel, (fields, levels, share, slot)),
        out_shape=(state, state),
        in_specs=[pl.BlockSpec(memory_space=pltpu.SMEM)] + [any_space] * 4,
        out_specs=(any_space, any_space),
        scratch_shapes=[
            whole,
            vmem((2 * levels * tiles, LANES), F32),
            whole,
            whole,
            whole,
            *[vmem((PIECES * slot * tiles, LANES), F32)] * 4,
            *[vmem((2 * chans, LANES), F32)] * 4,
            *[vmem((2 * levels, LANES), F32)] * 2,
            *[vmem((2, 2 * chans, LANES), F32)] * 2,
            vmem((4, 8 * (fields + 1), LANES), F32),
            vmem((4, 8 * fields, LANES), F32),
            vmem((PIECES, 144, SPAN), F32),
            vmem((PIECES, ROWS, SPAN), F32),
            vmem((ROWS, BLOCK, PIECES * BLOCK), BF16),
            vmem((ROWS, BLOCK, PIECES * BLOCK), BF16),
            vmem((PIECES, slot, cells), BF16),
            vmem((PIECES, slot, cells), BF16),
            vmem((PIECES, slot, cells), F32),
            dma((9,)),
            *[dma((PIECES,))] * 8,
            dma((2, 2)),
            dma((2, 2)),
            dma((3, 2)),
            dma((3, 2)),
        ],
        compiler_params=pltpu.CompilerParams(
            collective_id=0, has_side_effects=True, vmem_limit_bytes=60 * 1024 * 1024
        ),
    )(
        cutoff,
        jnp.asarray(table),
        tangent.reshape(chans * tiles, LANES),
        adjoint.reshape(chans * tiles, LANES),
        winds.reshape(2 * levels * tiles, LANES),
    )
    return tl.reshape(tangent.shape), adj.reshape(tangent.shape)


def solution(mesh):
    band = P(None, None, "lat", "lon")
    return jax.shard_map(
        shards, mesh=mesh, in_specs=(band, band, band, P()), out_specs=(band, band), check_vma=False
    )
```

profile of v0, /device:TPU:1, one launch (start us, length us, event | category | flops | bytes accessed | tf_op | source)
XLA Modules:
  0.0 91.9 jit_solution(7816829077219622642)
XLA Ops:
  0.6 86.2 %shard_map.68 = (f32[3240,128]{1,0:T(8,128)}, f32[3240,128]{1,0:T(8,128)}) custom-call(s32[128]{0:T(128)} %cut_ref.1, f32[8,144,512]{2,1,0:T(8,128)} %constant.2.clone.table_hbm, f32[3240,128]{1,0:T(8,128)} %bitcast.5, f32[3240,128]{1,0:T(8,128)} %bitcast.6, f32[1296,128]{1,0:T(8,128)} %bitcast.9), custom_call_target="tpu_custom_call" | custom-call | tf_op jit(solution)/shard_map/pallas_call | solution.py:472
  86.8 0.0 copy-start
  86.8 3.9 %copy.11 = f32[5,72,1,1152]{3,2,1,0:T(1,128)} copy(f32[5,72,1,1152]{3,2,1,0:T(1,128)} %bitcast.8) | data formatting | bytes 3317760
  90.7 0.0 copy-done
  90.7 1.2 %copy.12 = f32[5,72,1,1152]{3,2,1,0:T(1,128)} copy(f32[5,72,1,1152]{3,2,1,0:T(1,128)S(1)} %bitcast.7) | data formatting | bytes 3317760
Async XLA Ops:
  86.8 3.9 %copy-start = (f32[3240,128]{1,0:T(8,128)S(1)}, f32[3240,128]{1,0:T(8,128)}, u32[]{:S(2)}) copy-start(f32[3240,128]{1,0:T(8,128)} %get-tuple-element.5) | copy-start | bytes 4976644
where the time goes:
time: 92 us; the launch traced here: 91.9 us
  Pallas kernels  86.2 us (94%)
  local copies, waits for them, and re-layouts  5.04 us (5%)
    pallas_call x1, Pallas kernels, shards(): pl.pallas_call(functools.partial(kernel, (fields, levels, share, slot)),...  86.2 us
    unnamed x4, local copies, waits for them, and re-layouts  5.04 us

commit v1 on v0

--- a/solution.py
+++ b/solution.py
@@ -19,6 +19,8 @@
 SPAN = 512
 KINDS = (0, 4, 1, 2, 3)
 ORDER = (4, 3, 5, 2, 6, 1, 7)
+FIRST = 2
+PARTS = 1
 ROOT = math.sqrt(0.5)
 
 
@@ -76,7 +78,6 @@
     wind_v,
     moved_v,
     damped_v,
-    result_v,
     got_a,
     got_t,
     back_a,
@@ -111,6 +112,8 @@
     edge_recv,
     row_send,
     row_recv,
+    cycle_sem,
+    bands_sem,
 ):
     fields, levels, share, slot = dims
     chans = fields * levels
@@ -122,17 +125,20 @@
     bands = lax.axis_size("lat")
     west, east = lax.rem(me + PIECES - 1, PIECES), lax.rem(me + 1, PIECES)
     south, north = lax.rem(band + bands - 1, bands), lax.rem(band + 1, bands)
+    has_south, has_north = band > 0, band < bands - 1
     lane = lax.broadcasted_iota(jnp.int32, (8, LANES), 1)
     in16 = lane % 16
     sub = lane // 16
 
     barrier = pltpu.get_barrier_semaphore()
-    for step in range(1, PIECES):
-        pl.semaphore_signal(
-            barrier, inc=1, device_id={"lon": lax.rem(me + step, PIECES)}, device_id_type=MESH
-        )
-    for other in (south, north):
-        pl.semaphore_signal(barrier, inc=1, device_id={"lat": other}, device_id_type=MESH)
+    core = lax.rem(me, 2)
+    mate = me + 1 - 2 * core
+    for step in range(0, PIECES, 2):
+        @pl.when((step > 0) | (core == 1))
+        def _():
+            pl.semaphore_signal(
+                barrier, inc=1, device_id={"lon": lax.rem(me - core + step, PIECES)}, device_id_type=MESH
+            )
 
     load_tan = pltpu.make_async_copy(tan_hbm, tan_v, local_sem.at[0])
     load_wind = pltpu.make_async_copy(wind_hbm, wind_v, local_sem.at[1])
@@ -153,13 +159,15 @@
 
         def body(lg, carry):
             first, last = list(carry[0]), list(carry[1])
+            rest = [jnp.zeros((8, LANES), F32)] * 2
             for f in range(planes):
                 if f < fields:
                     at = (f * groups + lg) * 8
                     t = [tile_of(source, at * tiles + k) for k in range(tiles)]
-                    for k in range(2):
-                        line[0, pl.ds(k * chans + at, 8), :] = t[k]
-                        line[1, pl.ds(k * chans + at, 8), :] = t[k + tiles - 2]
+                    line[0, pl.ds(at, 8), :] = t[0]
+                    line[1, pl.ds(at, 8), :] = t[tiles - 1]
+                    rest[0] = jnp.where(sub == f, pltpu.roll(t[1], 16 * f, 1), rest[0])
+                    rest[1] = jnp.where(sub == f, pltpu.roll(t[tiles - 2], 16 * f + 16, 1), rest[1])
                 else:
                     t = [tile_of(wind, lg * 8 * tiles + k) for k in range(tiles)]
                     for k in range(2):
@@ -173,6 +181,8 @@
                 here = in16 == lg
                 first[f] = jnp.where(here, pltpu.roll(a, lg, 1), first[f])
                 last[f] = jnp.where(here, pltpu.roll(b, lg + (LANES - 15), 1), last[f])
+            for k in range(2):
+                line[k, pl.ds(chans + lg * 8, 8), :] = rest[k]
             return tuple(first), tuple(last)
 
         zero = tuple(jnp.zeros((8, LANES), F32) for _ in range(planes))
@@ -205,9 +215,21 @@
             ),
         ]
 
+    def start_rows(copies):
+        pl.when(has_south)(copies[0].start)
+        pl.when(has_north)(copies[1].start)
+
+    def wait_rows(copies):
+        pl.when(has_north)(copies[0].wait_recv)
+        pl.when(has_south)(copies[1].wait_recv)
+
+    def sent_rows(copies):
+        pl.when(has_south)(copies[0].wait_send)
+        pl.when(has_north)(copies[1].wait_send)
+
     def stencil(source, edge, from_south, from_north, target, sign):
-        has_south = jnp.where(band > 0, 0.5, 0.0).astype(F32)
-        has_north = jnp.where(band < bands - 1, 0.5, 0.0).astype(F32)
+        half_south = jnp.where(has_south, 0.5, 0.0).astype(F32)
+        half_north = jnp.where(has_north, 0.5, 0.0).astype(F32)
 
         def left(x, n):
             return pltpu.roll(x, LANES - n, 1)
@@ -215,9 +237,11 @@
         def body(lg, _):
             u = [tile_of(wind_v, lg * 8 * tiles + k) * 0.5 for k in range(tiles)]
             v = [tile_of(wind_v, (groups + lg) * 8 * tiles + k) for k in range(tiles)]
-            v = [x * 0.5 for x in v[:-2]] + [v[-2] * jnp.where(lane >= 112, has_north, 0.5), v[-1] * has_north]
-            v = [south_w[pl.ds(k * levels + lg * 8, 8), :] * has_south for k in range(2)] + v
+            v = [x * 0.5 for x in v[:-2]] + [v[-2] * jnp.where(lane >= 112, half_north, 0.5), v[-1] * half_north]
+            v = [south_w[pl.ds(k * levels + lg * 8, 8), :] * half_south for k in range(2)] + v
             u_west = pltpu.roll(edge_t[2, 8 * fields : 8 * fields + 8, :], LANES - lg, 1) * 0.5
+            rest_south = from_south[pl.ds(chans + lg * 8, 8), :]
+            rest_north = from_north[pl.ds(chans + lg * 8, 8), :]
             for f in range(fields):
                 at = (f * groups + lg) * 8
                 t = [tile_of(source, at * tiles + k) for k in range(tiles)]
@@ -237,9 +261,9 @@
                     if k < ROWS:
                         prev = jnp.where(lane == 16 * k, u_west * (far_west + sign * t[k]), prev)
                     out.append(t[k] - flux[k] + sign * prev)
-                ext = [from_south[pl.ds(k * chans + at, 8), :] for k in range(2)] + t
-                ext = ext + [from_north[pl.ds(k * chans + at, 8), :] for k in range(2)]
-                shifted = [left(x, 16) for x in ext]
+                ext = [pltpu.roll(rest_south, 112 - 16 * f, 1), from_south[pl.ds(at, 8), :]] + t
+                ext = ext + [from_north[pl.ds(at, 8), :]]
+                shifted = [left(x, 16) for x in ext] + [pltpu.roll(rest_north, 112 - 16 * f, 1)]
                 flux = []
                 for k in range(tiles + 2):
                     nxt = jnp.where(lane < 112, shifted[k + 1], shifted[k + 2])
@@ -381,31 +405,60 @@
         for c in copies:
             c.wait_send()
 
+    @pl.when(core == 0)
+    def _():
+        pl.semaphore_wait(barrier, PIECES - 1)
+        pl.semaphore_signal(cycle_sem, inc=1, device_id={"lon": mate}, device_id_type=MESH)
+
+    @pl.when(core == 1)
+    def _():
+        pl.semaphore_wait(cycle_sem, 1)
+        for there, other in ((has_south, south), (has_north, north)):
+
+            @pl.when(there)
+            def _(other=other):
+                pl.semaphore_signal(barrier, inc=1, device_id={"lat": other}, device_id_type=MESH)
+
+    @pl.when(band == 0)
+    def _():
+        south_t[...] = jnp.zeros_like(south_t)
+        south_d[...] = jnp.zeros_like(south_d)
+        south_w[...] = jnp.zeros_like(south_w)
+
+    @pl.when(band == bands - 1)
+    def _():
+        north_t[...] = jnp.zeros_like(north_t)
+        north_d[...] = jnp.zeros_like(north_d)
+
+    send_a = scatter(adj_hbm, got_a, fwd_a_send, fwd_a_recv)
+    start(send_a[:FIRST])
     load_tan.wait()
     load_wind.wait()
-    pack(
-        tan_v, wind_v, edge_t, line_t
-    )
-    pl.semaphore_wait(barrier, PIECES + 1)
-
+    pack(tan_v, wind_v, edge_t, line_t)
     edges_t = edges(edge_t, 0)
     start(edges_t)
-    send_a = scatter(adj_hbm, got_a, fwd_a_send, fwd_a_recv)
-    start(send_a)
+    start(send_a[FIRST:])
+
+    @pl.when(core == 1)
+    def _():
+        pl.semaphore_wait(barrier, jnp.where(has_south & has_north, 2, 1))
+        pl.semaphore_signal(bands_sem, inc=1, device_id={"lon": mate}, device_id_type=MESH)
+
+    @pl.when(core == 0)
+    def _():
+        pl.semaphore_wait(bands_sem, 1)
+
     rows_t = rows(line_t, north_t, south_t, 0)
     rows_w = pltpu.make_async_remote_copy(
         wind_row, south_w,
         row_send.at[2, 0], row_recv.at[2, 0], device_id={"lat": north}, device_id_type=MESH,
     )
-    start(rows_t)
-    rows_w.start()
-
-    load_table.wait()
-    matrices()
+    start_rows(rows_t)
+    pl.when(has_north)(rows_w.start)
 
     wait_recv(edges_t)
-    wait_recv(rows_t)
-    rows_w.wait_recv()
+    wait_rows(rows_t)
+    pl.when(has_south)(rows_w.wait_recv)
     stencil(tan_v, edge_t, south_t, north_t, moved_v, 1.0)
     send_t = scatter(moved_v, got_t, fwd_t_send, fwd_t_recv)
     start(send_t)
@@ -414,6 +467,8 @@
     )
     own_t.start()
 
+    load_table.wait()
+    matrices()
     own_a.wait()
     wait_recv(send_a)
     damp(got_a, back_a)
@@ -428,32 +483,45 @@
     wait_recv(send_t)
     damp(got_t, back_t)
 
+    home_t = bring(back_t, tl_out, back_t_send, back_t_recv)
+    start(home_t[:FIRST])
     keep_a.wait()
     wait_recv(home_a)
     pack(damped_v, None, edge_d, line_d)
     edges_d = edges(edge_d, 1)
     start(edges_d)
     rows_d = rows(line_d, north_d, south_d, 1)
-    start(rows_d)
-    home_t = bring(back_t, tl_out, back_t_send, back_t_recv)
-    start(home_t)
+    start_rows(rows_d)
+    start(home_t[FIRST:])
     keep_t = pltpu.make_async_copy(
         back_t.at[pl.ds(me * room, size)], tl_out.at[pl.ds(me * size, size)], local_sem.at[7]
     )
     keep_t.start()
 
     wait_recv(edges_d)
-    wait_recv(rows_d)
-    stencil(damped_v, edge_d, south_d, north_d, result_v, -1.0)
-    store = pltpu.make_async_copy(result_v, adj_out, local_sem.at[8])
-    store.start()
-
-    for copies in (edges_t, send_a, rows_t, send_t, home_a, edges_d, rows_d):
+    wait_rows(rows_d)
+    stencil(damped_v, edge_d, south_d, north_d, adj_out, -1.0)
+
+    for copies in (edges_t, send_a, send_t, home_a, edges_d):
         wait_send(copies)
-    rows_w.wait_send()
+    sent_rows(rows_t)
+    sent_rows(rows_d)
+    pl.when(has_north)(rows_w.wait_send)
     keep_t.wait()
-    store.wait()
     for c in home_t:
+        c.wait()
+
+
+def store(tl_ref, adj_ref, tl_out, adj_out, sem):
+    rows = tl_ref.shape[0] // PARTS
+    copies = []
+    for k, (source, target) in enumerate(((tl_ref, tl_out), (adj_ref, adj_out))):
+        for p in range(PARTS):
+            here = pl.ds(p * rows, rows)
+            copies.append(pltpu.make_async_copy(source.at[here], target.at[here], sem.at[k, p]))
+    for c in copies:
+        c.start()
+    for c in copies:
         c.wait()
 
 
@@ -464,26 +532,24 @@
     slot = -(-share // 16) * 16
     tiles = cells // LANES
     table = split_table(PIECES * cells // ROWS)
-    state = jax.ShapeDtypeStruct((chans * tiles, LANES), F32)
     any_space = pl.BlockSpec(memory_space=pl.ANY)
     vmem = pltpu.VMEM
     dma = pltpu.SemaphoreType.DMA
     whole = vmem((chans * tiles, LANES), F32)
     tl, adj = pl.pallas_call(
         functools.partial(kernel, (fields, levels, share, slot)),
-        out_shape=(state, state),
+        out_shape=(whole, whole),
         in_specs=[pl.BlockSpec(memory_space=pltpu.SMEM)] + [any_space] * 4,
-        out_specs=(any_space, any_space),
+        out_specs=(pl.BlockSpec(memory_space=pltpu.VMEM),) * 2,
         scratch_shapes=[
             whole,
             vmem((2 * levels * tiles, LANES), F32),
             whole,
             whole,
-            whole,
             *[vmem((PIECES * slot * tiles, LANES), F32)] * 4,
-            *[vmem((2 * chans, LANES), F32)] * 4,
+            *[vmem((chans + levels, LANES), F32)] * 4,
             *[vmem((2 * levels, LANES), F32)] * 2,
-            *[vmem((2, 2 * chans, LANES), F32)] * 2,
+            *[vmem((2, chans + levels, LANES), F32)] * 2,
             vmem((4, 8 * (fields + 1), LANES), F32),
             vmem((4, 8 * fields, LANES), F32),
             vmem((PIECES, 144, SPAN), F32),
@@ -493,15 +559,17 @@
             vmem((PIECES, slot, cells), BF16),
             vmem((PIECES, slot, cells), BF16),
             vmem((PIECES, slot, cells), F32),
-            dma((9,)),
+            dma((8,)),
             *[dma((PIECES,))] * 8,
             dma((2, 2)),
             dma((2, 2)),
             dma((3, 2)),
             dma((3, 2)),
+            pltpu.SemaphoreType.REGULAR,
+            pltpu.SemaphoreType.REGULAR,
         ],
         compiler_params=pltpu.CompilerParams(
-            collective_id=0, has_side_effects=True, vmem_limit_bytes=60 * 1024 * 1024
+            collective_id=0, has_side_effects=True, vmem_limit_bytes=62600000
         ),
     )(
         cutoff,
@@ -510,6 +578,14 @@
         adjoint.reshape(chans * tiles, LANES),
         winds.reshape(2 * levels * tiles, LANES),
     )
+    tl, adj = pl.pallas_call(
+        store,
+        out_shape=(jax.ShapeDtypeStruct((chans * tiles, LANES), F32),) * 2,
+        in_specs=[pl.BlockSpec(memory_space=pltpu.VMEM)] * 2,
+        out_specs=(any_space, any_space),
+        scratch_shapes=[dma((2, PARTS))],
+        compiler_params=pltpu.CompilerParams(vmem_limit_bytes=1024 * 1024),
+    )(tl, adj)
     return tl.reshape(tangent.shape), adj.reshape(tangent.shape)
 
 

time: 92 us -> 83.5 us (0.908); the launches traced: 91.9 us -> 82.3 us
  local copies, waits for them, and re-layouts: 5.04 us -> 0 us
  Pallas kernels: 86.2 us -> 81.7 us
    pallas_call x1, Pallas kernels: 86.2 us -> 80 us  [shards(): pl.pallas_call(functools.partial(kernel, (fields, levels, share, slot)),...]
    unnamed x4 -> x0, local copies, waits for them, and re-layouts: 5.04 us -> none
    pallas_call x0 -> x1, Pallas kernels: none -> 1.74 us  [shards(): pl.pallas_call(store, out_shape=(jax.ShapeDtypeStruct((chans * tiles, LAN...]
where the time goes in v1:
time: 83.5 us; the launch traced here: 82.3 us
  Pallas kernels  81.7 us (98%)
    pallas_call x1, Pallas kernels, shards(): pl.pallas_call(functools.partial(kernel, (fields, levels, share, slot)),...  80 us
    pallas_call x1, Pallas kernels, shards(): pl.pallas_call(store, out_shape=(jax.ShapeDtypeStruct((chans * tiles, LAN...  1.74 us

profile of v1, /device:TPU:1, one launch (start us, length us, event | category | flops | bytes accessed | tf_op | source)
XLA Modules:
  0.0 82.3 jit_solution(9335118130744391563)
XLA Ops:
  0.6 80.0 %shard_map.68 = (f32[3240,128]{1,0:T(8,128)S(1)}, f32[3240,128]{1,0:T(8,128)S(1)}) custom-call(s32[128]{0:T(128)} %cut_ref.1, f32[8,144,512]{2,1,0:T(8,128)} %constant.2.clone.table_hbm, f32[3240,128]{1,0:T(8,128)} %bitcast.5, f32[3240,128]{1,0:T(8,128)} %bitcast.6, f32[1296,128]{1,0:T(8,128)} %bitcast.7), custom_call_target="tpu_custom_call" | custom-call | tf_op jit(solution)/shard_map/pallas_call | solution.py:539
  80.6 1.7 %shard_map.69 = (f32[3240,128]{1,0:T(8,128)}, f32[3240,128]{1,0:T(8,128)}) custom-call(f32[3240,128]{1,0:T(8,128)S(1)} %get-tuple-element.6.tl_ref, f32[3240,128]{1,0:T(8,128)S(1)} %get-tuple-element.7.adj_ref), custom_call_target="tpu_custom_call" | custom-call | tf_op jit(solution)/shard_map/pallas_call | solution.py:581

commit v2 on v1

--- a/solution.py
+++ b/solution.py
@@ -18,8 +18,11 @@
 BLOCK = 256
 SPAN = 512
 KINDS = (0, 4, 1, 2, 3)
-ORDER = (4, 3, 5, 2, 6, 1, 7)
+ORDER = ((1, 0), (3, 0), (2, 0), (2, 1), (1, 1), (3, 1), (0, 1))
+NEAR = [k for k, (ahead, _) in enumerate(ORDER) if ahead != 2]
+FAR = [k for k, (ahead, _) in enumerate(ORDER) if ahead == 2]
 FIRST = 2
+PAD = 8
 PARTS = 1
 ROOT = math.sqrt(0.5)
 
@@ -133,15 +136,20 @@
     barrier = pltpu.get_barrier_semaphore()
     core = lax.rem(me, 2)
     mate = me + 1 - 2 * core
-    for step in range(0, PIECES, 2):
-        @pl.when((step > 0) | (core == 1))
-        def _():
-            pl.semaphore_signal(
-                barrier, inc=1, device_id={"lon": lax.rem(me - core + step, PIECES)}, device_id_type=MESH
-            )
-
-    load_tan = pltpu.make_async_copy(tan_hbm, tan_v, local_sem.at[0])
-    load_wind = pltpu.make_async_copy(wind_hbm, wind_v, local_sem.at[1])
+
+    def device(ahead, flip):
+        return lax.rem(me - core + 2 * ahead, PIECES) + (core if flip == 0 else 1 - core)
+
+    def tell(semaphore, axis, other):
+        pl.semaphore_signal(semaphore, inc=1, device_id={axis: other}, device_id_type=MESH)
+
+    for ahead in (1, 3):
+        tell(barrier, "lon", lax.rem(me - core + 2 * ahead, PIECES))
+    tell(barrier, "lon", lax.rem(me - core + 4, PIECES) + 1)
+    pl.when(core == 1)(lambda: tell(barrier, "lon", mate))
+
+    load_tan = pltpu.make_async_copy(tan_hbm, tan_v.at[pl.ds(0, chans * tiles)], local_sem.at[0])
+    load_wind = pltpu.make_async_copy(wind_hbm, wind_v.at[pl.ds(0, 2 * levels * tiles)], local_sem.at[1])
     load_table = pltpu.make_async_copy(table_hbm, table_v, local_sem.at[2])
     own_a = pltpu.make_async_copy(
         adj_hbm.at[pl.ds(me * size, size)], got_a.at[pl.ds(me * room, size)], local_sem.at[4]
@@ -371,8 +379,8 @@
 
     def scatter(source, got, send, recv):
         out = []
-        for step in ORDER:
-            to = lax.rem(me + step, PIECES)
+        for ahead, flip in ORDER:
+            to, step = device(ahead, flip), 2 * ahead + flip
             out.append(
                 pltpu.make_async_remote_copy(
                     source.at[pl.ds(to * size, size)], got.at[pl.ds(me * room, size)],
@@ -383,8 +391,8 @@
 
     def bring(back, target, send, recv):
         out = []
-        for step in ORDER:
-            to = lax.rem(me + step, PIECES)
+        for ahead, flip in ORDER:
+            to, step = device(ahead, flip), 2 * ahead + flip
             out.append(
                 pltpu.make_async_remote_copy(
                     back.at[pl.ds(to * room, size)], target.at[pl.ds(me * size, size)],
@@ -407,18 +415,17 @@
 
     @pl.when(core == 0)
     def _():
-        pl.semaphore_wait(barrier, PIECES - 1)
-        pl.semaphore_signal(cycle_sem, inc=1, device_id={"lon": mate}, device_id_type=MESH)
+        pl.semaphore_wait(barrier, 5)
+        tell(cycle_sem, "lon", mate)
 
     @pl.when(core == 1)
     def _():
         pl.semaphore_wait(cycle_sem, 1)
-        for there, other in ((has_south, south), (has_north, north)):
-
-            @pl.when(there)
-            def _(other=other):
-                pl.semaphore_signal(barrier, inc=1, device_id={"lat": other}, device_id_type=MESH)
-
+        pl.when(has_south)(lambda: tell(barrier, "lat", south))
+        pl.when(has_north)(lambda: tell(barrier, "lat", north))
+
+    send_a = scatter(adj_hbm, got_a, fwd_a_send, fwd_a_recv)
+    start(send_a[k] for k in NEAR[:2])
     @pl.when(band == 0)
     def _():
         south_t[...] = jnp.zeros_like(south_t)
@@ -430,24 +437,23 @@
         north_t[...] = jnp.zeros_like(north_t)
         north_d[...] = jnp.zeros_like(north_d)
 
-    send_a = scatter(adj_hbm, got_a, fwd_a_send, fwd_a_recv)
-    start(send_a[:FIRST])
     load_tan.wait()
     load_wind.wait()
     pack(tan_v, wind_v, edge_t, line_t)
     edges_t = edges(edge_t, 0)
     start(edges_t)
-    start(send_a[FIRST:])
+    start(send_a[k] for k in NEAR[2:])
 
     @pl.when(core == 1)
     def _():
-        pl.semaphore_wait(barrier, jnp.where(has_south & has_north, 2, 1))
-        pl.semaphore_signal(bands_sem, inc=1, device_id={"lon": mate}, device_id_type=MESH)
+        pl.semaphore_wait(barrier, jnp.where(has_south & has_north, 4, 3))
+        tell(bands_sem, "lon", mate)
 
     @pl.when(core == 0)
     def _():
         pl.semaphore_wait(bands_sem, 1)
 
+    start(send_a[k] for k in FAR)
     rows_t = rows(line_t, north_t, south_t, 0)
     rows_w = pltpu.make_async_remote_copy(
         wind_row, south_w,
@@ -513,7 +519,7 @@
 
 
 def store(tl_ref, adj_ref, tl_out, adj_out, sem):
-    rows = tl_ref.shape[0] // PARTS
+    rows = tl_out.shape[0] // PARTS
     copies = []
     for k, (source, target) in enumerate(((tl_ref, tl_out), (adj_ref, adj_out))):
         for p in range(PARTS):
@@ -535,18 +541,18 @@
     any_space = pl.BlockSpec(memory_space=pl.ANY)
     vmem = pltpu.VMEM
     dma = pltpu.SemaphoreType.DMA
-    whole = vmem((chans * tiles, LANES), F32)
+    whole = vmem((chans * tiles + PAD, LANES), F32)
     tl, adj = pl.pallas_call(
         functools.partial(kernel, (fields, levels, share, slot)),
-        out_shape=(whole, whole),
+        out_shape=(vmem((chans * tiles, LANES), F32), whole),
         in_specs=[pl.BlockSpec(memory_space=pltpu.SMEM)] + [any_space] * 4,
         out_specs=(pl.BlockSpec(memory_space=pltpu.VMEM),) * 2,
         scratch_shapes=[
             whole,
-            vmem((2 * levels * tiles, LANES), F32),
+            vmem((2 * levels * tiles + PAD, LANES), F32),
             whole,
             whole,
-            *[vmem((PIECES * slot * tiles, LANES), F32)] * 4,
+            *[vmem((PIECES * slot * tiles + PAD, LANES), F32)] * 4,
             *[vmem((chans + levels, LANES), F32)] * 4,
             *[vmem((2 * levels, LANES), F32)] * 2,
             *[vmem((2, chans + levels, LANES), F32)] * 2,

time: 83.5 us -> 82.8 us (level); the launches traced: 82.3 us -> 82.6 us
  no operation moved by 1% of the time
where the time goes in v2:
time: 82.8 us; the launch traced here: 82.6 us
  Pallas kernels  82 us (99%)
    pallas_call x1, Pallas kernels, shards(): pl.pallas_call(functools.partial(kernel, (fields, levels, share, slot)),...  80.2 us
    pallas_call x1, Pallas kernels, shards(): pl.pallas_call(store, out_shape=(jax.ShapeDtypeStruct((chans * tiles, LAN...  1.74 us

profile of v2, /device:TPU:1, one launch (start us, length us, event | category | flops | bytes accessed | tf_op | source)
XLA Modules:
  0.0 82.6 jit_solution(16611686220650293783)
XLA Ops:
  0.6 80.2 %shard_map.68 = (f32[3240,128]{1,0:T(8,128)S(1)}, f32[3248,128]{1,0:T(8,128)S(1)}) custom-call(s32[128]{0:T(128)} %cut_ref.1, f32[8,144,512]{2,1,0:T(8,128)} %constant.2.clone.table_hbm, f32[3240,128]{1,0:T(8,128)} %bitcast.5, f32[3240,128]{1,0:T(8,128)} %bitcast.6, f32[1296,128]{1,0:T(8,128)} %bitcast.7), custom_call_target="tpu_custom_call" | custom-call | tf_op jit(solution)/shard_map/pallas_call | solution.py:545
  80.9 1.7 %shard_map.69 = (f32[3240,128]{1,0:T(8,128)}, f32[3240,128]{1,0:T(8,128)}) custom-call(f32[3240,128]{1,0:T(8,128)S(1)} %get-tuple-element.6.tl_ref, f32[3248,128]{1,0:T(8,128)S(1)} %get-tuple-element.7.adj_ref), custom_call_target="tpu_custom_call" | custom-call | tf_op jit(solution)/shard_map/pallas_call | solution.py:587

commit v3 on v2

--- a/solution.py
+++ b/solution.py
@@ -413,6 +413,17 @@
         for c in copies:
             c.wait_send()
 
+    @pl.when(band == 0)
+    def _():
+        south_t[...] = jnp.zeros_like(south_t)
+        south_d[...] = jnp.zeros_like(south_d)
+        south_w[...] = jnp.zeros_like(south_w)
+
+    @pl.when(band == bands - 1)
+    def _():
+        north_t[...] = jnp.zeros_like(north_t)
+        north_d[...] = jnp.zeros_like(north_d)
+
     @pl.when(core == 0)
     def _():
         pl.semaphore_wait(barrier, 5)
@@ -426,17 +437,6 @@
 
     send_a = scatter(adj_hbm, got_a, fwd_a_send, fwd_a_recv)
     start(send_a[k] for k in NEAR[:2])
-    @pl.when(band == 0)
-    def _():
-        south_t[...] = jnp.zeros_like(south_t)
-        south_d[...] = jnp.zeros_like(south_d)
-        south_w[...] = jnp.zeros_like(south_w)
-
-    @pl.when(band == bands - 1)
-    def _():
-        north_t[...] = jnp.zeros_like(north_t)
-        north_d[...] = jnp.zeros_like(north_d)
-
     load_tan.wait()
     load_wind.wait()
     pack(tan_v, wind_v, edge_t, line_t)

time: 82.8 us -> 82.8 us (level)
  no operation moved by 1% of the time
where the time goes in v3:
time: 82.8 us; the launch traced here: 82.6 us
  Pallas kernels  82 us (99%)
    pallas_call x1, Pallas kernels, shards(): pl.pallas_call(functools.partial(kernel, (fields, levels, share, slot)),...  80.2 us
    pallas_call x1, Pallas kernels, shards(): pl.pallas_call(store, out_shape=(jax.ShapeDtypeStruct((chans * tiles, LAN...  1.74 us

profile of v3, /device:TPU:1, one launch (start us, length us, event | category | flops | bytes accessed | tf_op | source)
XLA Modules:
  0.0 82.6 jit_solution(1492451065448847742)
XLA Ops:
  0.6 80.2 %shard_map.68 = (f32[3240,128]{1,0:T(8,128)S(1)}, f32[3248,128]{1,0:T(8,128)S(1)}) custom-call(s32[128]{0:T(128)} %cut_ref.1, f32[8,144,512]{2,1,0:T(8,128)} %constant.2.clone.table_hbm, f32[3240,128]{1,0:T(8,128)} %bitcast.5, f32[3240,128]{1,0:T(8,128)} %bitcast.6, f32[1296,128]{1,0:T(8,128)} %bitcast.7), custom_call_target="tpu_custom_call" | custom-call | tf_op jit(solution)/shard_map/pallas_call | solution.py:545
  80.9 1.7 %shard_map.69 = (f32[3240,128]{1,0:T(8,128)}, f32[3240,128]{1,0:T(8,128)}) custom-call(f32[3240,128]{1,0:T(8,128)S(1)} %get-tuple-element.6.tl_ref, f32[3248,128]{1,0:T(8,128)S(1)} %get-tuple-element.7.adj_ref), custom_call_target="tpu_custom_call" | custom-call | tf_op jit(solution)/shard_map/pallas_call | solution.py:587
